TPU v7x, 32 devices: a whole 2x2x4 slice. The times are simulated.
32 devices in a mesh: grp: 4 (over z), rd: 8 (over y, x, core).
Axes of the slice: x: 2, y: 2, z: 4, core: 2. Of those that a mesh axis runs over, the one named last changes fastest.
Arguments:
- label_scores: bfloat16 [32768, 512], P(('grp', 'rd')), may hold values from -6 to 6
- degree: float32 [32768], P(('grp', 'rd')), may hold values from 1 to 4
- seed_label: int32 [8192], P(('grp', 'rd')), may hold values from 0 to 1023
- wanted: int32 [4, 8, 8, 2], P('grp', 'rd'), may hold values from -1 to 3, as said below
- nbr_slot: int32 [4, 8, 4, 24], P('grp', 'rd'), may hold values from 0 to 15, as said below
- tiles: bfloat16 [4, 8, 4, 24, 256, 256], P('grp', 'rd'), may hold values from 0 to 0.025512695
Outputs:
- new_scores: float32 [8192, 512], P(('grp', 'rd'))
Inputs may be any that keep to these rules, and one draw needn't show every extreme that they name: `wanted`: for each reader and each device of its column group, the live slots come first and hold distinct block indices of that device; each reader takes one or more blocks from every device of its group and exactly 2 from some device; -1 marks an empty slot. `nbr_slot`: each entry is the number s * 2 + c of a live slot of the same column group and reader in wanted; every live slot is named at least once.
All inputs are finite; a program needn't handle non-finite values.
Results may differ from a plain program's by a relative error of at most 0.0029.
Values may be sent and summed in bfloat16 or wider, within the bound.
A program may use at most 192 MiB of HBM per device.

v0:
```python
import jax
import jax.numpy as jnp
from jax import lax
from jax.sharding import PartitionSpec as P


def per_device(label_scores, degree, seed_label, wanted, nbr_slot, tiles):
    tile_rows = tiles.shape[-1]
    classes = label_scores.shape[1]
    owned = label_scores.shape[0] // tile_rows
    readers = lax.axis_size("rd")
    my_wanted = wanted[0, 0]
    slot_ids = nbr_slot[0, 0]
    my_tiles = tiles[0, 0]
    neighbours = slot_ids.shape[1]
    scaled = (label_scores * lax.rsqrt(degree)[:, None]).astype(jnp.bfloat16)
    gathered = lax.all_gather(scaled, "rd", axis=0, tiled=True)
    fetch_pool = gathered.reshape(readers * owned, tile_rows, classes)
    source_block = jnp.arange(readers, dtype=jnp.int32)[:, None] * owned + jnp.maximum(my_wanted, 0)
    flat_source = source_block.reshape(-1)
    match = slot_ids[..., None] == jnp.arange(flat_source.shape[0], dtype=jnp.int32)
    block_index = jnp.sum(jnp.where(match, flat_source, 0), axis=-1)
    out_count = tile_rows * lax.axis_size("grp") // tile_rows
    fetched = jnp.take(fetch_pool, block_index.reshape(-1), axis=0)
    fetched = fetched.reshape(out_count, neighbours, tile_rows, classes)
    product = jnp.einsum("qkij,qkjc->qic", my_tiles, fetched, preferred_element_type=jnp.float32)
    spread = lax.psum_scatter(
        product.reshape(tile_rows * lax.axis_size("grp"), classes),
        "grp",
        scatter_dimension=0,
        tiled=True,
    )
    degree_out = degree[:tile_rows]
    onehot = (seed_label[:, None] == jnp.arange(classes, dtype=jnp.int32)[None, :]).astype(
        jnp.float32
    )
    return 0.8 * lax.rsqrt(degree_out)[:, None] * spread + 0.2 * onehot


def solution(mesh):
    in_specs = (
        P(("grp", "rd"), None),
        P(("grp", "rd")),
        P(("grp", "rd")),
        P("grp", "rd", None, None),
        P("grp", "rd", None, None),
        P("grp", "rd", None, None, None, None),
    )
    out_specs = P(("grp", "rd"), None)
    return jax.shard_map(
        per_device, mesh=mesh, in_specs=in_specs, out_specs=out_specs, check_vma=False
    )
```

profile of v0, /device:TPU:0, one launch (start us, length us, event | category | flops | bytes accessed | tf_op | source)
XLA Modules:
  0.0 150.0 jit_solution(8846728880116830132)
XLA Ops:
  6.5 0.0 all-gather.2.cloned.1.call-start
  6.5 0.7 rsqrt.7
  7.2 2.5 %multiply_convert_fusion = bf16[1024,512]{1,0:T(8,128)(2,1)} fusion(bf16[1024,512]{1,0:T(8,128)(2,1)} %param.6, f32[1024]{0:T(1024)S(1)} %rsqrt.7), kind=kLoop, calls=%fused_computation.6 | loop fusion | flops 1572864 | bytes 2101248 | tf_op jit(solution)/shard_map/convert_element_type | solution.py:16
  9.7 0.0 all-gather.2.cloned.1.call-update
  9.7 0.0 reduce-scatter.2.cloned.1.call-start
  9.8 0.7 broadcast_maximum_fusion
  10.5 0.1 copy.9
  10.6 0.1 max.8
  10.6 0.1 add.38
  10.7 0.1 add.39
  10.8 0.8 select_reduce_fusion
  11.6 0.1 reshape.62
  11.7 55.3 %all-gather.2.cloned.1.call-done = bf16[8192,512]{1,0:T(8,128)(2,1)} async-done(((bf16[1024,512]{1,0:T(8,128)(2,1)}), bf16[8192,512]{1,0:T(8,128)(2,1)}) %all-gather.2.cloned.1.call-update) | async-done | bytes 8388624 | tf_op jit(solution)/shard_map/all_gather | solution.py:17
  67.0 13.6 %gather_fusion = bf16[96,256,512]{2,1,0:T(8,128)(2,1)} fusion(bf16[32,256,512]{2,1,0:T(8,128)(2,1)} %bitcast.16, s32[1024]{0:T(1024)S(1)} %pad_clamp_fusion), kind=kCustom, calls=%fused_computation | custom fusion | bytes 50332032 | tf_op jit(solution)/shard_map/jit(_take)/gather | solution.py:24
  80.6 0.0 copy-start
  80.6 16.6 %fusion = f32[4,512,256,1]{1,2,3,0:T(8,128)} fusion(bf16[4,24,256,512]{3,2,1,0:T(8,128)(2,1)} %bitcast.17, pred[4,24]{1,0:T(4,128)(4,1)S(1)} %compare_and_fusion, bf16[1,1,4,24,256,256]{5,4,3,2,1,0:T(8,128)(2,1)} %param.11), kind=kOutput, calls=%fused_computation.1 | convolution fusion | flops 6455033856 | bytes 39845984 | tf_op jit(solution)/shard_map/qkij,qkjc->qic/dot_general | solution.py:26
  97.2 0.0 reduce-scatter.2.cloned.1.call-update
  97.2 0.7 rsqrt_multiply_fusion
  97.9 43.3 %reduce-scatter.2.cloned.1.call-done = f32[256,512]{1,0:T(8,128)} async-done(((f32[1024,512]{1,0:T(8,128)}), f32[256,512]{1,0:T(8,128)}) %reduce-scatter.2.cloned.1.call-update) | async-done | bytes 524304 | tf_op jit(solution)/shard_map/reduce_scatter | solution.py:27
  141.2 0.0 copy-done
  141.2 2.0 %select_add_fusion = f32[256,512]{1,0:T(8,128)} fusion(f32[256,512]{1,0:T(8,128)} %reduce-scatter.2.cloned.1.call-done, s32[256]{0:T(256)S(1)} %copy-done, f32[256]{0:T(256)S(1)} %rsqrt_multiply_fusion), kind=kLoop, calls=%fused_computation.7 | loop fusion | flops 524288 | bytes 1050624 | tf_op jit(solution)/shard_map/add | solution.py:37
  (5 shorter events, 0.0 us)
Async XLA Ops:
  6.5 60.5 %all-gather.2.cloned.1.call-start = ((), (), s32[]{:S(2)}) async-start(), calls=%async_computation.1 | async-start | bytes 9437184 | tf_op jit(solution)/shard_map/all_gather | solution.py:17
  9.7 131.5 %reduce-scatter.2.cloned.1.call-start = ((), (), s32[]{:S(2)}) async-start(), calls=%async_computation.2 | async-start | bytes 2621440 | tf_op jit(solution)/shard_map/reduce_scatter | solution.py:27
  80.6 60.6 %copy-start = (s32[256]{0:T(256)S(1)}, s32[256]{0:T(256)}, u32[]{:S(2)}) copy-start(s32[256]{0:T(256)} %param.8) | copy-start | bytes 3076
Sparse Core Ops, SparseCore 0:
  9.9 57.0 all-gather.1
  97.4 43.8 reduce-scatter.1
where the time goes:
time: 150 us
  waiting for transfers between devices  98.6 us (66%)
  matrix products  16.6 us (11%)
  local copies, waits for them, and re-layouts  14.7 us (10%)
  between operations  13.4 us (9%)
  other arithmetic  6.65 us (4%)
    all_gather x1, waiting for transfers between devices, per_device(): gathered = lax.all_gather(scaled, 'rd', axis=0, tiled=True)  55.3 us
    reduce_scatter x1, waiting for transfers between devices, per_device(): lax.psum_scatter(product.reshape(tile_rows * lax.axis_size('grp'), classe...  43.3 us
    dot_general x1, matrix products, per_device(): jnp.einsum('qkij,qkjc->qic', my_tiles, fetched, preferred_element_type=jn...  16.6 us
    gather x1, local copies, waits for them, and re-layouts, per_device(): fetched = jnp.take(fetch_pool, block_index.reshape(-1), axis=0)  13.6 us
  transfers between devices with their start and end apart: 2, of which 2 were waited for; matrix products, arithmetic and copies ran while one was open for 2% of the time, Pallas kernels for 0%

commit v1 on v0

v1 whole, which is shorter than its diff:
```python
import functools
import math

import jax
import jax.numpy as jnp
from jax import lax
from jax.experimental import pallas as pl
from jax.experimental.pallas import tpu as pltpu
from jax.sharding import PartitionSpec as P

MESH_ID = pl.DeviceIdType.MESH
CHUNK = 128
UNROLL = 8


def spread_kernel(
    dims, labels, degree, wanted, slots, tiles_hbm, out, *scratch
):
    groups, y_size, x_size, own, rows, near, chunks, cap = dims
    pool = scratch[:chunks]
    sent = scratch[chunks : 2 * chunks]
    landed = scratch[2 * chunks : 3 * chunks]
    tiles, tile_sem, x_send, x_recv, y_send, y_recv, s_send, s_recv, z_send, z_recv = scratch[
        3 * chunks :
    ]
    g = lax.axis_index("grp")
    me = lax.axis_index("rd")
    core = lax.rem(me, 2)
    x = lax.rem(lax.div(me, 2), x_size)
    y = lax.div(me, 2 * x_size)
    half = own // 2

    def device(yy, xx, cc):
        return (yy * x_size + xx) * 2 + cc

    def x_at(step):
        return lax.rem(x + step, x_size)

    def y_at(step):
        return lax.rem(y + step, y_size)

    sibling = device(y, x, 1 - core)

    tile_copies = []
    for d in range(groups):
        q = lax.rem(g + d, groups)
        copy = pltpu.make_async_copy(
            tiles_hbm.at[0, 0, q], tiles.at[pl.ds(q * near, near)], tile_sem.at[d]
        )
        tile_copies.append(copy)

    barrier = pltpu.get_barrier_semaphore()
    peers = [(g, device(y, x_at(i), core)) for i in range(1, x_size)]
    peers += [(g, device(y_at(i), x, core)) for i in range(1, y_size)]
    peers += [(g, sibling)]
    peers += [(lax.rem(g + d, groups), me) for d in range(1, groups)]
    for peer in peers:
        pl.semaphore_signal(barrier, inc=1, device_id=peer, device_id_type=MESH_ID)
    for copy in tile_copies:
        copy.start()

    lanes = 128
    eye = lax.broadcasted_iota(jnp.int32, (lanes, lanes), 0) == lax.broadcasted_iota(
        jnp.int32, (lanes, lanes), 1
    )

    def scale(part, carry):
        row = degree[pl.ds(part, 1), :]
        column = jnp.sum(
            jnp.where(eye, jnp.broadcast_to(row, (lanes, lanes)), 0.0), axis=1, keepdims=True
        )
        factor = lax.rsqrt(column)
        per_block = rows // lanes
        block = me * own + lax.div(part, per_block)
        first = lax.rem(part, per_block) * lanes
        for c in range(chunks):
            piece = labels[pl.ds(part * lanes, lanes), c * CHUNK : (c + 1) * CHUNK]
            pool[c][block, pl.ds(first, lanes), :] = (
                piece.astype(jnp.float32) * factor
            ).astype(jnp.bfloat16)
        return carry

    lax.fori_loop(0, own * rows // lanes, scale, 0)
    pl.semaphore_wait(barrier, len(peers))

    pending = []

    def copy_of(c, first, count, send, recv, target):
        view = pool[c].at[pl.ds(first, count)]
        return pltpu.make_async_remote_copy(
            src_ref=view,
            dst_ref=view,
            send_sem=send,
            recv_sem=recv,
            device_id=target,
            device_id_type=MESH_ID,
        )

    def x_copy(c, i, j, which, source, target):
        return copy_of(
            c,
            source * own + which * half,
            half,
            x_send.at[c, i, j, which],
            x_recv.at[c, i, j, which],
            (g, target),
        )

    def y_copy(c, i, j, which, source, target):
        return copy_of(
            c,
            source * own + which * half,
            half,
            y_send.at[c, i, j, which],
            y_recv.at[c, i, j, which],
            (g, target),
        )

    def s_copy(c, i, j, source):
        return copy_of(
            c, source * own, own, s_send.at[c, i, j], s_recv.at[c, i, j], (g, sibling)
        )

    def start(copy):
        copy.start()
        pending.append(copy)

    def send_own(c):
        for which in (0, 1):
            for j in range(1, x_size):
                start(x_copy(c, 0, j, which, me, device(y, x_at(j), core)))
            for i in range(1, y_size):
                start(y_copy(c, i, 0, 1 - which, me, device(y_at(i), x, core)))
        start(s_copy(c, 0, 0, me))

    def forward(c):
        for j in range(1, x_size):
            source = device(y, x_at(x_size - j), core)
            x_copy(c, 0, j, 0, source, sibling).wait_recv()
            for i in range(1, y_size):
                start(y_copy(c, i, j, 0, source, device(y_at(i), x, core)))
        for i in range(1, y_size):
            source = device(y_at(y_size - i), x, core)
            y_copy(c, i, 0, 1, source, sibling).wait_recv()
            for j in range(1, x_size):
                start(x_copy(c, i, j, 1, source, device(y, x_at(j), core)))

    def complete(c):
        for j in range(1, x_size):
            source = device(y, x_at(x_size - j), core)
            x_copy(c, 0, j, 1, source, sibling).wait_recv()
            start(s_copy(c, 0, j, source))
        for i in range(1, y_size):
            source = device(y_at(y_size - i), x, core)
            y_copy(c, i, 0, 0, source, sibling).wait_recv()
            start(s_copy(c, i, 0, source))
        for i in range(1, y_size):
            for j in range(1, x_size):
                source = device(y_at(y_size - i), x_at(x_size - j), core)
                y_copy(c, i, j, 0, source, sibling).wait_recv()
                x_copy(c, i, j, 1, source, sibling).wait_recv()
                start(s_copy(c, i, j, source))
        for i in range(y_size):
            for j in range(x_size):
                source = device(y_at(y_size - i), x_at(x_size - j), 1 - core)
                s_copy(c, i, j, source).wait_recv()

    def block_of(q, k):
        slot = slots[0, 0, q, k]
        source = lax.div(slot, cap)
        local = wanted[0, 0, source, lax.rem(slot, cap)]
        return source * own + jnp.maximum(local, 0)

    def z_copy(c, d):
        return pltpu.make_async_remote_copy(
            src_ref=sent[c].at[d - 1],
            dst_ref=landed[c].at[d - 1],
            send_sem=z_send.at[c, d - 1],
            recv_sem=z_recv.at[c, d - 1],
            device_id=(lax.rem(g + d, groups), me),
            device_id_type=MESH_ID,
        )

    order = sorted(range(1, groups), key=lambda d: abs(d - groups / 2)) + [0]

    def compute(c):
        for d in order:
            if c == 0:
                tile_copies[d].wait()
            q = lax.rem(g + d, groups)

            def body(step, acc):
                ks = [step * UNROLL + u for u in range(UNROLL)]
                left = jnp.concatenate([tiles[q * near + k] for k in ks], axis=1)
                right = jnp.concatenate([pool[c][block_of(q, k)] for k in ks], axis=0)
                return acc + jnp.dot(left, right, preferred_element_type=jnp.float32)

            acc = lax.fori_loop(
                0, near // UNROLL, body, jnp.zeros((rows, CHUNK), jnp.float32)
            )
            if d == 0:
                out[:, c * CHUNK : (c + 1) * CHUNK] = acc
            else:
                sent[c][d - 1] = acc.astype(jnp.bfloat16)
                start(z_copy(c, d))

    def finish(c):
        total = out[:, c * CHUNK : (c + 1) * CHUNK]
        for d in order[:-1]:
            z_copy(c, d).wait_recv()
            total = total + landed[c][d - 1].astype(jnp.float32)
        out[:, c * CHUNK : (c + 1) * CHUNK] = total

    send_own(0)
    if chunks > 1:
        send_own(1)
    forward(0)
    for c in range(chunks):
        if c + 2 < chunks:
            send_own(c + 2)
        if c + 1 < chunks:
            forward(c + 1)
        complete(c)
        compute(c)
    for c in range(chunks):
        finish(c)
    for copy in pending:
        copy.wait_send()


def per_device(groups, readers, label_scores, degree, seed_label, wanted, nbr_slot, tiles):
    rows = tiles.shape[-1]
    classes = label_scores.shape[1]
    own = label_scores.shape[0] // rows
    near = nbr_slot.shape[-1]
    cap = wanted.shape[-1]
    chunks = classes // CHUNK
    chips = readers // 2
    x_size = math.isqrt(chips)
    y_size = chips // x_size
    dims = (groups, y_size, x_size, own, rows, near, chunks, cap)
    dma = pltpu.SemaphoreType.DMA
    vmem = pl.BlockSpec(memory_space=pltpu.VMEM)
    smem = pl.BlockSpec(memory_space=pltpu.SMEM)
    spread = pl.pallas_call(
        functools.partial(spread_kernel, dims),
        out_shape=jax.ShapeDtypeStruct((rows, classes), jnp.float32),
        in_specs=[vmem, vmem, smem, smem, pl.BlockSpec(memory_space=pl.ANY)],
        out_specs=vmem,
        scratch_shapes=[
            pltpu.VMEM((readers * own, rows, CHUNK), jnp.bfloat16) for _ in range(chunks)
        ]
        + [pltpu.VMEM((groups - 1, rows, CHUNK), jnp.bfloat16) for _ in range(2 * chunks)]
        + [
            pltpu.VMEM((groups * near, rows, rows), jnp.bfloat16),
            dma((groups,)),
            dma((chunks, y_size, x_size, 2)),
            dma((chunks, y_size, x_size, 2)),
            dma((chunks, y_size, x_size, 2)),
            dma((chunks, y_size, x_size, 2)),
            dma((chunks, y_size, x_size)),
            dma((chunks, y_size, x_size)),
            dma((chunks, groups - 1)),
            dma((chunks, groups - 1)),
        ],
        compiler_params=pltpu.CompilerParams(
            collective_id=0, has_side_effects=True, vmem_limit_bytes=60 * 1024 * 1024
        ),
    )(label_scores, degree.reshape(-1, 128), wanted, nbr_slot, tiles)
    degree_out = degree[:rows]
    onehot = (seed_label[:, None] == jnp.arange(classes, dtype=jnp.int32)[None, :]).astype(
        jnp.float32
    )
    return 0.8 * lax.rsqrt(degree_out)[:, None] * spread + 0.2 * onehot


def solution(mesh):
    in_specs = (
        P(("grp", "rd"), None),
        P(("grp", "rd")),
        P(("grp", "rd")),
        P("grp", "rd", None, None),
        P("grp", "rd", None, None),
        P("grp", "rd", None, None, None, None),
    )
    out_specs = P(("grp", "rd"), None)
    body = functools.partial(per_device, mesh.shape["grp"], mesh.shape["rd"])
    return jax.shard_map(
        body, mesh=mesh, in_specs=in_specs, out_specs=out_specs, check_vma=False
    )
```

time: 150 us -> 64 us (0.43)
  waiting for transfers between devices: 98.6 us -> 0 us
  Pallas kernels: 0 us -> 59.7 us
  matrix products: 16.6 us -> 0 us
  between operations: 13.4 us -> 0.01 us
  local copies, waits for them, and re-layouts: 14.7 us -> 1.36 us
  other arithmetic: 6.65 us -> 2.67 us
    pallas_call x0 -> x1, Pallas kernels: none -> 59.7 us  [per_device(): pl.pallas_call(functools.partial(spread_kernel, dims), out_shape=jax.Shap...]
    all_gather x1 -> x0, waiting for transfers between devices: 55.3 us -> none  [per_device(): gathered = lax.all_gather(scaled, 'rd', axis=0, tiled=True)]
    reduce_scatter x1 -> x0, waiting for transfers between devices: 43.3 us -> none  [per_device(): lax.psum_scatter(product.reshape(tile_rows * lax.axis_size('grp'), classe...]
    dot_general x1 -> x0, matrix products: 16.6 us -> none  [per_device(): jnp.einsum('qkij,qkjc->qic', my_tiles, fetched, preferred_element_type=jn...]
    gather x1 -> x0, local copies, waits for them, and re-layouts: 13.6 us -> none  [per_device(): fetched = jnp.take(fetch_pool, block_index.reshape(-1), axis=0)]
    convert_element_type x1 -> x0, other arithmetic: 2.49 us -> none  [per_device(): scaled = (label_scores * lax.rsqrt(degree)[:, None]).astype(jnp.bfloat16)]
  transfers between devices with their start and end apart: 2 -> 0, of which waited for: 2 -> 0; matrix products, arithmetic and copies ran while one was open for 2% -> 0% of each run, Pallas kernels for 0% -> 0%
where the time goes in v1:
time: 64 us; the launch traced here: 63.8 us
  Pallas kernels  59.7 us (93%)
  other arithmetic  2.67 us (4%)
  local copies, waits for them, and re-layouts  1.36 us (2%)
    pallas_call x1, Pallas kernels, per_device(): pl.pallas_call(functools.partial(spread_kernel, dims), out_shape=jax.Shap...  59.7 us
    add x1, other arithmetic, per_device(): return 0.8 * lax.rsqrt(degree_out)[:, None] * spread + 0.2 * onehot  1.98 us
    unnamed x3, local copies, waits for them, and re-layouts  1.36 us

profile of v1, /device:TPU:0, one launch (start us, length us, event | category | flops | bytes accessed | tf_op | source)
XLA Modules:
  0.0 63.8 jit_solution(4877633526303191531)
XLA Ops:
  0.0 0.0 copy-start
  0.0 1.4 %copy.7.wanted = s32[1,1,8,2]{3,2,1,0:T(8,128)} copy(s32[1,1,8,2]{2,3,1,0:T(2,128)} %param.9) | data formatting | bytes 128 | tf_op args[3]
  1.4 59.7 %shard_map.64 = f32[256,512]{1,0:T(8,128)} custom-call(bf16[1024,512]{1,0:T(8,128)(2,1)} %labels.1, f32[8,128]{1,0:T(8,128)} %bitcast.1, s32[1,1,8,2]{3,2,1,0:T(8,128)} %copy.7.wanted, s32[1,1,4,24]{3,2,1,0:T(4,128)} %slots.1, bf16[1,1,4,24,256,256]{5,4,3,2,1,0:T(8,128)(2,1)} %tiles_hbm.1), custom_call_target="tpu_custom_call" | custom-call | tf_op jit(solution)/shard_map/pallas_call | solution.py:245
  61.1 0.7 %rsqrt_multiply_fusion = f32[256]{0:T(256)S(1)} fusion(f32[1024]{0:T(1024)} %param.7), kind=kLoop, calls=%fused_computation.2 | loop fusion | flops 256 | bytes 2048 | tf_op jit(solution)/shard_map/mul | solution.py:274
  61.8 0.0 copy-done
  61.8 2.0 %select_add_fusion = f32[256,512]{1,0:T(8,128)} fusion(f32[256,512]{1,0:T(8,128)} %shard_map.64, s32[256]{0:T(256)S(1)} %copy-done, f32[256]{0:T(256)S(1)} %rsqrt_multiply_fusion), kind=kLoop, calls=%fused_computation | loop fusion | flops 524288 | bytes 1050624 | tf_op jit(solution)/shard_map/add | solution.py:274
Async XLA Ops:
  0.0 61.8 %copy-start = (s32[256]{0:T(256)S(1)}, s32[256]{0:T(256)}, u32[]{:S(2)}) copy-start(s32[256]{0:T(256)} %param.8) | copy-start | bytes 3076

commit v2 on v1

--- a/solution.py
+++ b/solution.py
@@ -10,17 +10,17 @@
 
 MESH_ID = pl.DeviceIdType.MESH
 CHUNK = 128
-UNROLL = 8
+UNROLL = 24
 
 
 def spread_kernel(
-    dims, labels, degree, wanted, slots, tiles_hbm, out, *scratch
+    dims, labels, degree, seeds, wanted, slots, tiles_hbm, out, *scratch
 ):
     groups, y_size, x_size, own, rows, near, chunks, cap = dims
     pool = scratch[:chunks]
     sent = scratch[chunks : 2 * chunks]
     landed = scratch[2 * chunks : 3 * chunks]
-    tiles, tile_sem, x_send, x_recv, y_send, y_recv, s_send, s_recv, z_send, z_recv = scratch[
+    weight, seed_class, tiles, tile_sem, x_send, x_recv, y_send, y_recv, s_send, s_recv, z_send, z_recv = scratch[
         3 * chunks :
     ]
     g = lax.axis_index("grp")
@@ -64,23 +64,27 @@
         jnp.int32, (lanes, lanes), 1
     )
 
-    def scale(part, carry):
-        row = degree[pl.ds(part, 1), :]
-        column = jnp.sum(
-            jnp.where(eye, jnp.broadcast_to(row, (lanes, lanes)), 0.0), axis=1, keepdims=True
-        )
-        factor = lax.rsqrt(column)
-        per_block = rows // lanes
-        block = me * own + lax.div(part, per_block)
-        first = lax.rem(part, per_block) * lanes
-        for c in range(chunks):
-            piece = labels[pl.ds(part * lanes, lanes), c * CHUNK : (c + 1) * CHUNK]
-            pool[c][block, pl.ds(first, lanes), :] = (
-                piece.astype(jnp.float32) * factor
-            ).astype(jnp.bfloat16)
-        return carry
-
-    lax.fori_loop(0, own * rows // lanes, scale, 0)
+    def column_of(row):
+        spread_row = jnp.broadcast_to(row, (lanes, lanes))
+        return jnp.sum(jnp.where(eye, spread_row, 0.0), axis=1, keepdims=True)
+
+    per_block = rows // lanes
+
+    def scale(columns):
+        def body(part, carry):
+            factor = lax.rsqrt(column_of(degree[pl.ds(part, 1), :]))
+            block = me * own + lax.div(part, per_block)
+            first = lax.rem(part, per_block) * lanes
+            for c in columns:
+                piece = labels[pl.ds(part * lanes, lanes), c * CHUNK : (c + 1) * CHUNK]
+                pool[c][block, pl.ds(first, lanes), :] = (
+                    piece.astype(jnp.float32) * factor
+                ).astype(jnp.bfloat16)
+            return carry
+
+        lax.fori_loop(0, own * per_block, body, 0)
+
+    scale([0])
     pl.semaphore_wait(barrier, len(peers))
 
     pending = []
@@ -125,13 +129,13 @@
         copy.start()
         pending.append(copy)
 
-    def send_own(c):
-        for which in (0, 1):
-            for j in range(1, x_size):
-                start(x_copy(c, 0, j, which, me, device(y, x_at(j), core)))
-            for i in range(1, y_size):
-                start(y_copy(c, i, 0, 1 - which, me, device(y_at(i), x, core)))
-        start(s_copy(c, 0, 0, me))
+    def send_own(c, which):
+        for j in range(1, x_size):
+            start(x_copy(c, 0, j, which, me, device(y, x_at(j), core)))
+        for i in range(1, y_size):
+            start(y_copy(c, i, 0, 1 - which, me, device(y_at(i), x, core)))
+        if which == 0:
+            start(s_copy(c, 0, 0, me))
 
     def forward(c):
         for j in range(1, x_size):
@@ -168,7 +172,7 @@
     def block_of(q, k):
         slot = slots[0, 0, q, k]
         source = lax.div(slot, cap)
-        local = wanted[0, 0, source, lax.rem(slot, cap)]
+        local = wanted[0, 0, lax.rem(slot, cap), source]
         return source * own + jnp.maximum(local, 0)
 
     def z_copy(c, d):
@@ -181,12 +185,9 @@
             device_id_type=MESH_ID,
         )
 
-    order = sorted(range(1, groups), key=lambda d: abs(d - groups / 2)) + [0]
-
     def compute(c):
-        for d in order:
-            if c == 0:
-                tile_copies[d].wait()
+        def piece(i, carry):
+            d = lax.rem(i + 1, groups)
             q = lax.rem(g + d, groups)
 
             def body(step, acc):
@@ -195,34 +196,59 @@
                 right = jnp.concatenate([pool[c][block_of(q, k)] for k in ks], axis=0)
                 return acc + jnp.dot(left, right, preferred_element_type=jnp.float32)
 
-            acc = lax.fori_loop(
-                0, near // UNROLL, body, jnp.zeros((rows, CHUNK), jnp.float32)
-            )
-            if d == 0:
-                out[:, c * CHUNK : (c + 1) * CHUNK] = acc
+            acc = jnp.zeros((rows, CHUNK), jnp.float32)
+            if near == UNROLL:
+                acc = body(0, acc)
             else:
-                sent[c][d - 1] = acc.astype(jnp.bfloat16)
-                start(z_copy(c, d))
+                acc = lax.fori_loop(0, near // UNROLL, body, acc)
+            out[:, c * CHUNK : (c + 1) * CHUNK] = acc
+
+            @pl.when(i < groups - 1)
+            def _():
+                sent[c][i] = acc.astype(jnp.bfloat16)
+                z_copy(c, i + 1).start()
+
+            return carry
+
+        lax.fori_loop(0, groups, piece, 0)
+        pending.extend(z_copy(c, d) for d in range(1, groups))
 
     def finish(c):
         total = out[:, c * CHUNK : (c + 1) * CHUNK]
-        for d in order[:-1]:
+        for d in range(1, groups):
             z_copy(c, d).wait_recv()
             total = total + landed[c][d - 1].astype(jnp.float32)
-        out[:, c * CHUNK : (c + 1) * CHUNK] = total
-
-    send_own(0)
+        classes = c * CHUNK + lax.broadcasted_iota(jnp.int32, (rows, CHUNK), 1)
+        hit = jnp.where(seed_class[...] == classes, 1.0, 0.0)
+        out[:, c * CHUNK : (c + 1) * CHUNK] = weight[...] * total + 0.2 * hit
+
+    send_own(0, 0)
+    send_own(0, 1)
+    scale(range(1, chunks))
     if chunks > 1:
-        send_own(1)
+        send_own(1, 0)
     forward(0)
+    for part in range(per_block):
+        at = pl.ds(part * lanes, lanes)
+        factor = 0.8 * lax.rsqrt(column_of(degree[pl.ds(part, 1), :]))
+        weight[at, :] = jnp.broadcast_to(factor, (lanes, CHUNK))
+        label = column_of(seeds[pl.ds(part, 1), :].astype(jnp.float32))
+        seed_class[at, :] = jnp.broadcast_to(label, (lanes, CHUNK)).astype(jnp.int32)
     for c in range(chunks):
+        if c + 1 < chunks:
+            send_own(c + 1, 1)
         if c + 2 < chunks:
-            send_own(c + 2)
+            send_own(c + 2, 0)
         if c + 1 < chunks:
             forward(c + 1)
+        if c >= 2:
+            finish(c - 2)
         complete(c)
+        if c == 0:
+            for copy in tile_copies:
+                copy.wait()
         compute(c)
-    for c in range(chunks):
+    for c in range(max(chunks - 2, 0), chunks):
         finish(c)
     for copy in pending:
         copy.wait_send()
@@ -242,16 +268,18 @@
     dma = pltpu.SemaphoreType.DMA
     vmem = pl.BlockSpec(memory_space=pltpu.VMEM)
     smem = pl.BlockSpec(memory_space=pltpu.SMEM)
-    spread = pl.pallas_call(
+    return pl.pallas_call(
         functools.partial(spread_kernel, dims),
         out_shape=jax.ShapeDtypeStruct((rows, classes), jnp.float32),
-        in_specs=[vmem, vmem, smem, smem, pl.BlockSpec(memory_space=pl.ANY)],
+        in_specs=[vmem, vmem, vmem, smem, smem, pl.BlockSpec(memory_space=pl.ANY)],
         out_specs=vmem,
         scratch_shapes=[
             pltpu.VMEM((readers * own, rows, CHUNK), jnp.bfloat16) for _ in range(chunks)
         ]
         + [pltpu.VMEM((groups - 1, rows, CHUNK), jnp.bfloat16) for _ in range(2 * chunks)]
         + [
+            pltpu.VMEM((rows, CHUNK), jnp.float32),
+            pltpu.VMEM((rows, CHUNK), jnp.int32),
             pltpu.VMEM((groups * near, rows, rows), jnp.bfloat16),
             dma((groups,)),
             dma((chunks, y_size, x_size, 2)),
@@ -266,12 +294,14 @@
         compiler_params=pltpu.CompilerParams(
             collective_id=0, has_side_effects=True, vmem_limit_bytes=60 * 1024 * 1024
         ),
-    )(label_scores, degree.reshape(-1, 128), wanted, nbr_slot, tiles)
-    degree_out = degree[:rows]
-    onehot = (seed_label[:, None] == jnp.arange(classes, dtype=jnp.int32)[None, :]).astype(
-        jnp.float32
+    )(
+        label_scores,
+        degree.reshape(-1, 128),
+        seed_label.reshape(-1, 128),
+        jnp.swapaxes(wanted, 2, 3),
+        nbr_slot,
+        tiles,
     )
-    return 0.8 * lax.rsqrt(degree_out)[:, None] * spread + 0.2 * onehot
 
 
 def solution(mesh):

time: 64 us -> 55.9 us (0.87)
  Pallas kernels: 59.7 us -> 53.8 us
  other arithmetic: 2.67 us -> 0 us
    pallas_call x1, Pallas kernels: 59.7 us -> 53.8 us  [per_device(): pl.pallas_call(functools.partial(spread_kernel, dims), out_shape=jax.Shap...]
    add x1 -> x0, other arithmetic: 1.98 us -> none  [per_device(): return 0.8 * lax.rsqrt(degree_out)[:, None] * spread + 0.2 * onehot]
    mul x1 -> x0, other arithmetic: 0.69 us -> none  [per_device(): return 0.8 * lax.rsqrt(degree_out)[:, None] * spread + 0.2 * onehot]
    unnamed x3 -> x1, local copies, waits for them, and re-layouts: 1.36 us -> 1.87 us
where the time goes in v2:
time: 55.9 us; the launch traced here: 55.7 us
  Pallas kernels  53.8 us (96%)
  local copies, waits for them, and re-layouts  1.87 us (3%)
    pallas_call x1, Pallas kernels, per_device(): pl.pallas_call(functools.partial(spread_kernel, dims), out_shape=jax.Shap...  53.8 us
    unnamed x1, local copies, waits for them, and re-layouts  1.87 us

profile of v2, /device:TPU:0, one launch (start us, length us, event | category | flops | bytes accessed | tf_op | source)
XLA Modules:
  0.0 55.7 jit_solution(12142889380890685758)
XLA Ops:
  0.0 53.8 %shard_map.64 = f32[256,512]{1,0:T(8,128)} custom-call(bf16[1024,512]{1,0:T(8,128)(2,1)} %labels.1, f32[8,128]{1,0:T(8,128)} %bitcast.3, s32[2,128]{1,0:T(2,128)} %bitcast.4, s32[1,1,2,8]{3,2,1,0:T(2,128)} %bitcast.5, s32[1,1,4,24]{3,2,1,0:T(4,128)} %slots.1, bf16[1,1,4,24,256,256]{5,4,3,2,1,0:T(8,128)(2,1)} %tiles_hbm.1), custom_call_target="tpu_custom_call" | custom-call | tf_op jit(solution)/shard_map/pallas_call | solution.py:271
  53.8 1.9 %copy.8 = f32[256,512]{1,0:T(8,128)} copy(f32[256,512]{1,0:T(8,128)} %shard_map.64) | data formatting | bytes 1048576

commit v3 on v2

--- a/solution.py
+++ b/solution.py
@@ -11,6 +11,7 @@
 MESH_ID = pl.DeviceIdType.MESH
 CHUNK = 128
 UNROLL = 24
+SPLIT = 1
 
 
 def spread_kernel(
@@ -20,7 +21,7 @@
     pool = scratch[:chunks]
     sent = scratch[chunks : 2 * chunks]
     landed = scratch[2 * chunks : 3 * chunks]
-    weight, seed_class, tiles, tile_sem, x_send, x_recv, y_send, y_recv, s_send, s_recv, z_send, z_recv = scratch[
+    weight, seed_class, total_buf, label_buf, label_sem, out_sem, tiles, tile_sem, x_send, x_recv, y_send, y_recv, s_send, s_recv, z_send, z_recv = scratch[
         3 * chunks :
     ]
     g = lax.axis_index("grp")
@@ -56,7 +57,13 @@
     peers += [(lax.rem(g + d, groups), me) for d in range(1, groups)]
     for peer in peers:
         pl.semaphore_signal(barrier, inc=1, device_id=peer, device_id_type=MESH_ID)
-    for copy in tile_copies:
+    label_copies = [
+        pltpu.make_async_copy(
+            labels.at[:, pl.ds(c * CHUNK, CHUNK)], label_buf.at[c], label_sem.at[c]
+        )
+        for c in range(chunks)
+    ]
+    for copy in label_copies + tile_copies:
         copy.start()
 
     lanes = 128
@@ -71,12 +78,15 @@
     per_block = rows // lanes
 
     def scale(columns):
+        for c in columns:
+            label_copies[c].wait()
+
         def body(part, carry):
             factor = lax.rsqrt(column_of(degree[pl.ds(part, 1), :]))
             block = me * own + lax.div(part, per_block)
             first = lax.rem(part, per_block) * lanes
             for c in columns:
-                piece = labels[pl.ds(part * lanes, lanes), c * CHUNK : (c + 1) * CHUNK]
+                piece = label_buf[c, pl.ds(part * lanes, lanes), :]
                 pool[c][block, pl.ds(first, lanes), :] = (
                     piece.astype(jnp.float32) * factor
                 ).astype(jnp.bfloat16)
@@ -185,7 +195,7 @@
             device_id_type=MESH_ID,
         )
 
-    def compute(c):
+    def compute(c, low, high):
         def piece(i, carry):
             d = lax.rem(i + 1, groups)
             q = lax.rem(g + d, groups)
@@ -201,7 +211,7 @@
                 acc = body(0, acc)
             else:
                 acc = lax.fori_loop(0, near // UNROLL, body, acc)
-            out[:, c * CHUNK : (c + 1) * CHUNK] = acc
+            total_buf[c] = acc
 
             @pl.when(i < groups - 1)
             def _():
@@ -210,24 +220,32 @@
 
             return carry
 
-        lax.fori_loop(0, groups, piece, 0)
-        pending.extend(z_copy(c, d) for d in range(1, groups))
+        lax.fori_loop(low, high, piece, 0)
+
+    out_copies = [
+        pltpu.make_async_copy(
+            total_buf.at[c], out.at[:, pl.ds(c * CHUNK, CHUNK)], out_sem.at[c]
+        )
+        for c in range(chunks)
+    ]
 
     def finish(c):
-        total = out[:, c * CHUNK : (c + 1) * CHUNK]
+        total = total_buf[c]
         for d in range(1, groups):
             z_copy(c, d).wait_recv()
             total = total + landed[c][d - 1].astype(jnp.float32)
         classes = c * CHUNK + lax.broadcasted_iota(jnp.int32, (rows, CHUNK), 1)
         hit = jnp.where(seed_class[...] == classes, 1.0, 0.0)
-        out[:, c * CHUNK : (c + 1) * CHUNK] = weight[...] * total + 0.2 * hit
+        total_buf[c] = weight[...] * total + 0.2 * hit
+        out_copies[c].start()
 
     send_own(0, 0)
     send_own(0, 1)
     scale(range(1, chunks))
+    forward(0)
     if chunks > 1:
         send_own(1, 0)
-    forward(0)
+        send_own(1, 1)
     for part in range(per_block):
         at = pl.ds(part * lanes, lanes)
         factor = 0.8 * lax.rsqrt(column_of(degree[pl.ds(part, 1), :]))
@@ -235,23 +253,28 @@
         label = column_of(seeds[pl.ds(part, 1), :].astype(jnp.float32))
         seed_class[at, :] = jnp.broadcast_to(label, (lanes, CHUNK)).astype(jnp.int32)
     for c in range(chunks):
-        if c + 1 < chunks:
-            send_own(c + 1, 1)
-        if c + 2 < chunks:
-            send_own(c + 2, 0)
-        if c + 1 < chunks:
-            forward(c + 1)
-        if c >= 2:
-            finish(c - 2)
         complete(c)
         if c == 0:
             for copy in tile_copies:
                 copy.wait()
-        compute(c)
+        if c + 1 < chunks:
+            compute(c, 0, SPLIT)
+            forward(c + 1)
+            if c + 2 < chunks:
+                send_own(c + 2, 0)
+                send_own(c + 2, 1)
+            compute(c, SPLIT, groups)
+            if c >= 1:
+                finish(c - 1)
+        else:
+            compute(c, 0, groups)
+        pending.extend(z_copy(c, d) for d in range(1, groups))
     for c in range(max(chunks - 2, 0), chunks):
         finish(c)
     for copy in pending:
         copy.wait_send()
+    for copy in out_copies:
+        copy.wait()
 
 
 def per_device(groups, readers, label_scores, degree, seed_label, wanted, nbr_slot, tiles):
@@ -271,8 +294,8 @@
     return pl.pallas_call(
         functools.partial(spread_kernel, dims),
         out_shape=jax.ShapeDtypeStruct((rows, classes), jnp.float32),
-        in_specs=[vmem, vmem, vmem, smem, smem, pl.BlockSpec(memory_space=pl.ANY)],
-        out_specs=vmem,
+        in_specs=[pl.BlockSpec(memory_space=pl.ANY), vmem, vmem, smem, smem, pl.BlockSpec(memory_space=pl.ANY)],
+        out_specs=pl.BlockSpec(memory_space=pl.ANY),
         scratch_shapes=[
             pltpu.VMEM((readers * own, rows, CHUNK), jnp.bfloat16) for _ in range(chunks)
         ]
@@ -280,6 +303,10 @@
         + [
             pltpu.VMEM((rows, CHUNK), jnp.float32),
             pltpu.VMEM((rows, CHUNK), jnp.int32),
+            pltpu.VMEM((chunks, rows, CHUNK), jnp.float32),
+            pltpu.VMEM((chunks, own * rows, CHUNK), jnp.bfloat16),
+            dma((chunks,)),
+            dma((chunks,)),
             pltpu.VMEM((groups * near, rows, rows), jnp.bfloat16),
             dma((groups,)),
             dma((chunks, y_size, x_size, 2)),

time: 55.9 us -> 55.3 us (0.989)
  Pallas kernels: 53.8 us -> 53.2 us
    pallas_call x1, Pallas kernels: 53.8 us -> 53.2 us  [per_device(): pl.pallas_call(functools.partial(spread_kernel, dims), out_shape=jax.Shap...]
where the time goes in v3:
time: 55.3 us; the launch traced here: 55.1 us
  Pallas kernels  53.2 us (96%)
  local copies, waits for them, and re-layouts  1.87 us (3%)
    pallas_call x1, Pallas kernels, per_device(): pl.pallas_call(functools.partial(spread_kernel, dims), out_shape=jax.Shap...  53.2 us
    unnamed x1, local copies, waits for them, and re-layouts  1.87 us

profile of v3, /device:TPU:0, one launch (start us, length us, event | category | flops | bytes accessed | tf_op | source)
XLA Modules:
  0.0 55.1 jit_solution(16743031880616251375)
XLA Ops:
  0.0 53.2 %shard_map.64 = f32[256,512]{1,0:T(8,128)} custom-call(bf16[1024,512]{1,0:T(8,128)(2,1)} %labels.1, f32[8,128]{1,0:T(8,128)} %bitcast.3, s32[2,128]{1,0:T(2,128)} %bitcast.4, s32[1,1,2,8]{3,2,1,0:T(2,128)} %bitcast.5, s32[1,1,4,24]{3,2,1,0:T(4,128)} %slots.1, bf16[1,1,4,24,256,256]{5,4,3,2,1,0:T(8,128)(2,1)} %tiles_hbm.1), custom_call_target="tpu_custom_call" | custom-call | tf_op jit(solution)/shard_map/pallas_call | solution.py:294
  53.2 1.9 %copy.8 = f32[256,512]{1,0:T(8,128)} copy(f32[256,512]{1,0:T(8,128)} %shard_map.64) | data formatting | bytes 1048576

commit v4 on v3

--- a/solution.py
+++ b/solution.py
@@ -11,7 +11,7 @@
 MESH_ID = pl.DeviceIdType.MESH
 CHUNK = 128
 UNROLL = 24
-SPLIT = 1
+SPLIT = 0
 
 
 def spread_kernel(

time: 55.3 us -> 54.6 us (0.987)
  Pallas kernels: 53.2 us -> 52.5 us
    pallas_call x1, Pallas kernels: 53.2 us -> 52.5 us  [per_device(): pl.pallas_call(functools.partial(spread_kernel, dims), out_shape=jax.Shap...]
where the time goes in v4:
time: 54.6 us; the launch traced here: 54.4 us
  Pallas kernels  52.5 us (96%)
  local copies, waits for them, and re-layouts  1.87 us (3%)
    pallas_call x1, Pallas kernels, per_device(): pl.pallas_call(functools.partial(spread_kernel, dims), out_shape=jax.Shap...  52.5 us
    unnamed x1, local copies, waits for them, and re-layouts  1.87 us

profile of v4, /device:TPU:0, one launch (start us, length us, event | category | flops | bytes accessed | tf_op | source)
XLA Modules:
  0.0 54.4 jit_solution(6791954351873872557)
XLA Ops:
  0.0 52.5 %shard_map.64 = f32[256,512]{1,0:T(8,128)} custom-call(bf16[1024,512]{1,0:T(8,128)(2,1)} %labels.1, f32[8,128]{1,0:T(8,128)} %bitcast.3, s32[2,128]{1,0:T(2,128)} %bitcast.4, s32[1,1,2,8]{3,2,1,0:T(2,128)} %bitcast.5, s32[1,1,4,24]{3,2,1,0:T(4,128)} %slots.1, bf16[1,1,4,24,256,256]{5,4,3,2,1,0:T(8,128)(2,1)} %tiles_hbm.1), custom_call_target="tpu_custom_call" | custom-call | tf_op jit(solution)/shard_map/pallas_call | solution.py:294
  52.5 1.9 %copy.8 = f32[256,512]{1,0:T(8,128)} copy(f32[256,512]{1,0:T(8,128)} %shard_map.64) | data formatting | bytes 1048576
